TPU v7x, 32 devices: a whole 2x2x4 slice. The times are simulated.
32 devices in a mesh: dp: 4 (over y, x), mp: 8 (over z, core).
Axes of the slice: x: 2, y: 2, z: 4, core: 2. Of those that a mesh axis runs over, the one named last changes fastest.
Arguments:
- activations: bfloat16 [1024, 8192], P(('dp', 'mp')), may hold values from -6 to 6
- out_grads: bfloat16 [1024, 14336], P('dp', 'mp'), may hold values from -0.75 to 0.75
- basis: bfloat16 [8192, 512], P('mp'), may hold values from -0.0625 to 0.0625
- first_moment: float32 [512, 14336], P(None, 'mp'), may hold values from -3 to 3
- second_moment: float32 [512, 14336], P(None, 'mp'), may hold values from 0.0001 to 0.01
Outputs:
- update: bfloat16 [8192, 14336], P(None, 'mp')
- new_first: float32 [512, 14336], P(None, 'mp')
- new_second: float32 [512, 14336], P(None, 'mp')
All inputs are finite; a program needn't handle non-finite values.
Results may differ from a plain program's by a relative error of at most 0.0051.
Values may be sent and summed in bfloat16 or wider, within the bound.
A program may use at most 128 MiB of HBM per device.

v0:
```python
import jax
import jax.numpy as jnp
from jax import lax
from jax.sharding import PartitionSpec as P

STEP = 10


def body(activations, out_grads, basis, first_moment, second_moment):
    groups = lax.axis_size("dp")
    whole_basis = lax.all_gather(basis, "mp", axis=0, tiled=True)
    reduced = jnp.dot(activations, whole_basis, preferred_element_type=jnp.float32)
    group_reduced = lax.all_gather(reduced, "mp", axis=0, tiled=True)
    local_term = lax.dot_general(
        group_reduced,
        out_grads.astype(jnp.float32),
        (((0,), (0,)), ((), ())),
        precision=lax.Precision.HIGHEST,
        preferred_element_type=jnp.float32,
    )
    projected = lax.psum(local_term, "dp") / groups
    new_first = 0.9 * first_moment + 0.1 * projected
    new_second = 0.999 * second_moment + 0.001 * projected * projected
    first_hat = new_first / (1.0 - 0.9**STEP)
    second_hat = new_second / (1.0 - 0.999**STEP)
    normalized = (first_hat / (jnp.sqrt(second_hat) + 1e-08)).astype(jnp.bfloat16)
    update = jnp.dot(whole_basis, normalized, preferred_element_type=jnp.float32).astype(
        jnp.bfloat16
    )
    return (update, new_first, new_second)


def solution(mesh):
    return jax.shard_map(
        body,
        mesh=mesh,
        in_specs=(
            P(("dp", "mp"), None),
            P("dp", "mp"),
            P("mp", None),
            P(None, "mp"),
            P(None, "mp"),
        ),
        out_specs=(P(None, "mp"), P(None, "mp"), P(None, "mp")),
        check_vma=False,
    )
```

profile of v0, /device:TPU:1, one launch (start us, length us, event | category | flops | bytes accessed | tf_op | source)
XLA Modules:
  0.0 291.6 jit_solution(1920429838162815336)
XLA Ops:
  7.2 0.0 copy-start
  7.2 0.0 all-gather.2.cloned.1.call-start
  7.2 0.7 all-gather.2.cloned.1.call-update
  7.9 0.0 all-reduce.2.cloned.1.call-start
  8.0 86.2 %all-gather.2.cloned.1.call-done = bf16[8192,512]{1,0:T(8,128)(2,1)} async-done(((bf16[1024,512]{1,0:T(8,128)(2,1)}), bf16[8192,512]{1,0:T(8,128)(2,1)}) %all-gather.2.cloned.1.call-update) | async-done | bytes 8388624 | tf_op jit(solution)/shard_map/all_gather | solution.py:11
  94.2 5.1 %fusion.7 = f32[32,512]{1,0:T(8,128)S(1)} fusion(bf16[32,8192]{1,0:T(8,128)(2,1)} %param.5, bf16[8192,512]{1,0:T(8,128)(2,1)} %all-gather.2.cloned.1.call-done), kind=kOutput, calls=%fused_computation.11 | convolution fusion | flops 268435456 | bytes 8978432 | tf_op jit(solution)/shard_map/dot_general | solution.py:12
  99.3 14.9 %all_gather.7 = f32[256,512]{1,0:T(8,128)S(1)} all-gather(f32[32,512]{1,0:T(8,128)S(1)} %fusion.7), channel_id=1, replica_groups=mesh['dp'=4,'mp'=8] {'mp'}, dimensions={0}, use_global_device_ids=true | all-gather | bytes 589824 | tf_op jit(solution)/shard_map/all_gather | solution.py:13
  114.2 0.0 copy-done
  114.2 3.6 %fusion.8 = f32[512,1792]{1,0:T(8,128)} fusion(f32[256,512]{1,0:T(8,128)S(1)} %all_gather.7, bf16[256,1792]{1,0:T(8,128)(2,1)S(1)} %copy-done), kind=kOutput, calls=%fused_computation.12 | convolution fusion | flops 2818572288 | bytes 5111808 | tf_op jit(solution)/shard_map/dot_general | solution.py:14
  117.8 0.0 all-reduce.2.cloned.1.call-update
  117.8 94.0 %all-reduce.2.cloned.1.call-done = f32[512,1792]{1,0:T(8,128)} async-done(((f32[512,1792]{1,0:T(8,128)}), f32[512,1792]{1,0:T(8,128)}) %all-reduce.2.cloned.1.call-update) | async-done | bytes 3670032 | tf_op jit(solution)/shard_map/psum | solution.py:21
  211.8 8.4 %multiply_add_fusion.1 = (f32[512,1792]{1,0:T(8,128)}, f32[512,1792]{1,0:T(8,128)}) fusion(f32[512,1792]{1,0:T(8,128)} %all-reduce.2.cloned.1.call-done, f32[512,1792]{1,0:T(8,128)} %param.8, f32[512,1792]{1,0:T(8,128)} %param.9), kind=kLoop, calls=%fused_computation.4 | loop fusion | flops 7340032 | bytes 18350080 | tf_op jit(solution)/shard_map/add | solution.py:22
  220.2 28.6 %fusion = bf16[8192,1792]{0,1:T(8,128)(2,1)} fusion(bf16[8192,512]{1,0:T(8,128)(2,1)} %all-gather.2.cloned.1.call-done, f32[512,1792]{1,0:T(8,128)} %get-tuple-element.7, f32[512,1792]{1,0:T(8,128)} %get-tuple-element.6), kind=kOutput, calls=%fused_computation.1 | convolution fusion | flops 15051653120 | bytes 45088768 | tf_op jit(solution)/shard_map/dot_general | solution.py:27
  248.8 0.0 copy-start.1
  248.8 35.9 %copy.8 = bf16[8192,1792]{1,0:T(8,128)(2,1)} copy(bf16[8192,1792]{0,1:T(8,128)(2,1)} %fusion) | data formatting | bytes 58720256
  284.7 0.0 copy-done.1
Async XLA Ops:
  7.2 107.1 %copy-start = (bf16[256,1792]{1,0:T(8,128)(2,1)S(1)}, bf16[256,1792]{1,0:T(8,128)(2,1)}, u32[]{:S(2)}) copy-start(bf16[256,1792]{1,0:T(8,128)(2,1)} %param.6) | copy-start | bytes 2752516
  7.2 87.0 %all-gather.2.cloned.1.call-start = ((), (), s32[]{:S(2)}) async-start(), calls=%async_computation | async-start | bytes 9437184 | tf_op jit(solution)/shard_map/all_gather | solution.py:11
  7.9 203.9 %all-reduce.2.cloned.1.call-start = ((), (), s32[]{:S(2)}) async-start(), calls=%async_computation.1 | async-start | bytes 7340032 | tf_op jit(solution)/shard_map/psum | solution.py:21
  248.8 35.9 %copy-start.1 = (bf16[256,1792]{1,0:T(8,128)(2,1)S(1)}, bf16[256,1792]{1,0:T(8,128)(2,1)}, u32[]{:S(2)}) copy-start(bf16[256,1792]{1,0:T(8,128)(2,1)} %param.6) | copy-start | bytes 2752516
Sparse Core Ops, SparseCore 0:
  9.6 84.5 all-gather.1
  117.9 93.8 all-reduce.1
where the time goes:
time: 293 us; the launch traced here: 292 us
  waiting for transfers between devices  181 us (62%)
  matrix products  37.2 us (13%)
  local copies, waits for them, and re-layouts  35.9 us (12%)
  blocking collectives  14.9 us (5%)
  between operations  14 us (5%)
  other arithmetic  8.42 us (3%)
    psum x1, waiting for transfers between devices, body(): projected = lax.psum(local_term, 'dp') / groups  94 us
    all_gather x1, waiting for transfers between devices, body(): whole_basis = lax.all_gather(basis, 'mp', axis=0, tiled=True)  86.2 us
    unnamed x5, local copies, waits for them, and re-layouts  35.9 us
    dot_general x1, matrix products, body(): jnp.dot(whole_basis, normalized, preferred_element_type=jnp.float32)  28.6 us
    all_gather x1, blocking collectives, body(): group_reduced = lax.all_gather(reduced, 'mp', axis=0, tiled=True)  14.9 us
    add x1, other arithmetic, body(): new_first = 0.9 * first_moment + 0.1 * projected  8.42 us
  transfers between devices with their start and end apart: 2, of which 2 were waited for; matrix products, arithmetic and copies ran while one was open for 0% of the time, Pallas kernels for 0%

commit v1 on v0

v1 whole, which is shorter than its diff:
```python
import functools
import itertools

import jax
import jax.numpy as jnp
from jax import lax
from jax.experimental import pallas as pl
from jax.experimental.pallas import tpu as pltpu
from jax.sharding import PartitionSpec as P

STEP = 10
MESH = pl.DeviceIdType.MESH


def flip(index, stride):
    return index + stride - 2 * stride * lax.rem(lax.div(index, stride), 2)


def count_of(n_dp, n_mp):
    chips = n_mp // 2
    both = 2 * (n_dp - 1)
    return (chips - 1) * (2 + both) + 1 + both + (n_mp - 1) + both + (n_dp - 1)


def gather_kernel(
    n_dp, n_mp, act_ref, og_ref, basis_ref, basis_out, og_out, red_out,
    bas, og, red, acc, send, recv, local,
):
    q, m = lax.axis_index("dp"), lax.axis_index("mp")
    chips = n_mp // 2
    z, c = lax.div(m, 2), lax.rem(m, 2)
    twin = (q, 2 * z + 1 - c)
    strides = [1 << s for s in range(n_dp.bit_length() - 1)]
    orders = [strides, strides[::-1]]
    rows = basis_ref.shape[0]
    piece = rows // n_dp
    tokens = og_ref.shape[0]
    mine = act_ref.shape[0]

    barrier = pltpu.get_barrier_semaphore()
    for k in range(1, n_mp):
        pl.semaphore_signal(barrier, inc=1, device_id=(q, lax.rem(m + k, n_mp)), device_id_type=MESH)
    for stride in strides:
        pl.semaphore_signal(barrier, inc=1, device_id=(flip(q, stride), m), device_id_type=MESH)
    pl.semaphore_wait(barrier, n_mp - 1 + len(strides))

    numbers = itertools.count()
    sent = []

    def push(src, dst, device):
        i = next(numbers)
        copy = pltpu.make_async_remote_copy(
            src_ref=src, dst_ref=dst, send_sem=send.at[i], recv_sem=recv.at[i],
            device_id=device, device_id_type=MESH,
        )
        copy.start()
        sent.append(copy)
        return copy

    def part(ref, start, size):
        return ref.at[pl.ds(pl.multiple_of(start, 16), size), :]

    def stage(ref, base, step, size, half, held, s):
        stride = orders[half][s]
        partner = (flip(q, stride), m)
        copies = []
        for b in held:
            where = part(ref, base + b * step + half * size, size)
            copies.append(push(where, where, partner))
        return copies, held + [flip(b, stride) for b in held]

    def shard(k, core):
        return (2 * lax.rem(z - k + chips, chips) + core) * rows

    own = m * rows
    z_copies = []
    for k in range(1, chips):
        z_copies.append(push(
            part(basis_ref, q * piece, piece), part(bas, own + q * piece, piece),
            (q, 2 * lax.rem(z + k, chips) + c),
        ))
    twin_own = push(basis_ref, part(bas, own, rows), twin)

    og_half = tokens // 2
    og_held, og_copies = [[q], [q]], [[], []]
    for h in range(2):
        stride = orders[h][0]
        og_copies[h].append(push(
            part(og_ref, h * og_half, og_half), part(og, q * tokens + h * og_half, og_half),
            (flip(q, stride), m),
        ))
        og_held[h] = [q, flip(q, stride)]
    own_basis = pltpu.make_async_copy(basis_ref, part(bas, own, rows), local.at[0])
    own_basis.start()
    own_og = pltpu.make_async_copy(og_ref, part(og, q * tokens, tokens), local.at[1])
    own_og.start()

    def add(start):
        where = pl.multiple_of(start, 128)
        acc[...] += jnp.dot(
            act_ref[:, pl.ds(where, rows)], bas[pl.ds(where, rows), :],
            preferred_element_type=jnp.float32,
        )

    acc[...] = jnp.zeros_like(acc)
    own_basis.wait()
    add(own)

    half = piece // 2
    held = [[[q], [q]] for _ in range(chips)]
    flying = [[[], []] for _ in range(chips)]
    for s in range(len(strides)):
        for k in range(1, chips):
            base = shard(k, c)
            if s == 0:
                z_copies[k - 1].wait_recv()
            for h in range(2):
                for copy in flying[k][h]:
                    copy.wait_recv()
                flying[k][h], held[k][h] = stage(bas, base, piece, half, h, held[k][h], s)
    own_og.wait()
    for s in range(1, len(strides)):
        for h in range(2):
            for copy in og_copies[h]:
                copy.wait_recv()
            og_copies[h], og_held[h] = stage(og, 0, tokens, og_half, h, og_held[h], s)

    twin_own.wait_recv()
    add((2 * z + 1 - c) * rows)
    twin_copies = []
    for k in range(1, chips):
        base = shard(k, c)
        for h in range(2):
            for copy in flying[k][h]:
                copy.wait_recv()
        where = part(bas, base, rows)
        twin_copies.append(push(where, where, twin))
        add(base)
    for k in range(1, chips):
        twin_copies[k - 1].wait_recv()
        add(shard(k, 1 - c))

    place = q * tokens + m * mine
    red[pl.ds(pl.multiple_of(place, 16), mine), :] = acc[...].astype(red.dtype)
    group_copies = []
    for k in range(1, n_mp):
        where = part(red, place, mine)
        group_copies.append(push(where, where, (q, lax.rem(m + k, n_mp))))
    out_basis = pltpu.make_async_copy(bas, basis_out, local.at[2])
    out_basis.start()
    for copy in group_copies:
        copy.wait_recv()
    quarter = tokens // 4
    side = c * (tokens // 2)
    red_held, red_copies = [[q], [q]], [[], []]
    for s in range(len(strides)):
        for h in range(2):
            for copy in red_copies[h]:
                copy.wait_recv()
            red_copies[h], red_held[h] = stage(red, side, tokens, quarter, h, red_held[h], s)
    for h in range(2):
        for copy in red_copies[h]:
            copy.wait_recv()
    last = []
    for k in range(1, n_dp):
        where = part(red, lax.rem(q + k, n_dp) * tokens + side, tokens // 2)
        last.append(push(where, where, twin))
    for h in range(2):
        for copy in og_copies[h]:
            copy.wait_recv()
    out_og = pltpu.make_async_copy(og, og_out, local.at[3])
    out_og.start()
    for copy in last:
        copy.wait_recv()
    out_red = pltpu.make_async_copy(red, red_out, local.at[4])
    out_red.start()
    for copy in sent:
        copy.wait_send()
    out_basis.wait()
    out_og.wait()
    out_red.wait()


def gather(activations, out_grads, basis):
    n_dp, n_mp = lax.axis_size("dp"), lax.axis_size("mp")
    mine, width = activations.shape
    tokens, columns = out_grads.shape
    rank = basis.shape[1]
    count = count_of(n_dp, n_mp)
    anywhere = pl.BlockSpec(memory_space=pl.ANY)
    shapes = [(width, rank), (n_dp * tokens, columns), (n_dp * tokens, rank)]
    return pl.pallas_call(
        functools.partial(gather_kernel, n_dp, n_mp),
        out_shape=[jax.ShapeDtypeStruct(shape, jnp.bfloat16) for shape in shapes],
        in_specs=[pl.BlockSpec(memory_space=pltpu.VMEM), anywhere, anywhere],
        out_specs=[anywhere] * 3,
        scratch_shapes=[pltpu.VMEM(shape, jnp.bfloat16) for shape in shapes]
        + [
            pltpu.VMEM((mine, rank), jnp.float32),
            pltpu.SemaphoreType.DMA((count,)),
            pltpu.SemaphoreType.DMA((count,)),
            pltpu.SemaphoreType.DMA((5,)),
        ],
        compiler_params=pltpu.CompilerParams(
            collective_id=0, has_side_effects=True, vmem_limit_bytes=40 * 2**20
        ),
        name="gather",
    )(activations, out_grads, basis)


def step_kernel(
    groups, basis_ref, red_ref, og_ref, first_ref, second_ref, update_ref, new_first_ref,
    new_second_ref, turned,
):
    @pl.when(pl.program_id(0) == 0)
    def _():
        turned[...] = red_ref[...].T

    projected = jnp.dot(turned[...], og_ref[...], preferred_element_type=jnp.float32) / groups
    new_first = 0.9 * first_ref[...] + 0.1 * projected
    new_second = 0.999 * second_ref[...] + 0.001 * projected * projected
    new_first_ref[...] = new_first
    new_second_ref[...] = new_second
    first_hat = new_first / (1.0 - 0.9**STEP)
    second_hat = new_second / (1.0 - 0.999**STEP)
    normalized = (first_hat / (jnp.sqrt(second_hat) + 1e-08)).astype(jnp.bfloat16)
    rows = basis_ref.shape[0]
    chunk = min(rows, 1024)

    def one(i, carry):
        where = pl.ds(pl.multiple_of(i * chunk, chunk), chunk)
        update_ref[where, :] = jnp.dot(
            basis_ref[where, :], normalized, preferred_element_type=jnp.float32
        ).astype(update_ref.dtype)
        return carry

    lax.fori_loop(0, rows // chunk, one, 0)


def step(basis, red, og, first, second, groups):
    rank, columns = first.shape
    width, tokens = basis.shape[0], og.shape[0]
    block = 256 if columns % 256 == 0 else 128
    whole = lambda shape: pl.BlockSpec(shape, lambda j: (0, 0), pipeline_mode=pl.Buffered(1))
    column = lambda n: pl.BlockSpec((n, block), lambda j: (0, j))
    return pl.pallas_call(
        functools.partial(step_kernel, groups),
        grid=(columns // block,),
        out_shape=[
            jax.ShapeDtypeStruct((width, columns), jnp.bfloat16),
            jax.ShapeDtypeStruct(first.shape, jnp.float32),
            jax.ShapeDtypeStruct(second.shape, jnp.float32),
        ],
        in_specs=[
            whole((width, rank)), whole((tokens, rank)), column(tokens), column(rank), column(rank)
        ],
        out_specs=[column(width), column(rank), column(rank)],
        scratch_shapes=[pltpu.VMEM((rank, tokens), jnp.bfloat16)],
        compiler_params=pltpu.CompilerParams(vmem_limit_bytes=48 * 2**20),
        name="step",
    )(basis, red, og, first, second)


def body(activations, out_grads, basis, first_moment, second_moment):
    whole_basis, whole_grads, reduced = gather(activations, out_grads, basis)
    return tuple(step(
        whole_basis, reduced, whole_grads, first_moment, second_moment, lax.axis_size("dp")
    ))


def solution(mesh):
    return jax.shard_map(
        body,
        mesh=mesh,
        in_specs=(
            P(("dp", "mp"), None),
            P("dp", "mp"),
            P("mp", None),
            P(None, "mp"),
            P(None, "mp"),
        ),
        out_specs=(P(None, "mp"), P(None, "mp"), P(None, "mp")),
        check_vma=False,
    )
```

time: 293 us -> 120 us (0.41)
  the two profiles are of different devices: /device:TPU:1 before, /device:TPU:25 now
where the time goes in v1:
time: 120 us
  Pallas kernels  116 us (97%)
  local copies, waits for them, and re-layouts  3.44 us (3%)
    pallas_call x1, Pallas kernels, gather(): pl.pallas_call(functools.partial(gather_kernel, n_dp, n_mp), out_shape=[j...  79.3 us
    pallas_call x1, Pallas kernels, step(): pl.pallas_call(functools.partial(step_kernel, groups), grid=(columns // b...  36.6 us
    unnamed x6, local copies, waits for them, and re-layouts  3.44 us

profile of v1, /device:TPU:25, one launch (start us, length us, event | category | flops | bytes accessed | tf_op | source)
XLA Modules:
  0.0 120.0 jit_solution(5816438923004876835)
XLA Ops:
  0.6 0.0 copy-start
  0.6 1.2 %copy-done = bf16[1024,512]{1,0:T(8,128)(2,1)S(1)} copy-done((bf16[1024,512]{1,0:T(8,128)(2,1)S(1)}, bf16[1024,512]{1,0:T(8,128)(2,1)}, u32[]{:S(2)}) %copy-start) | copy-done | bytes 1048600
  1.9 0.0 copy-start.1
  1.9 1.2 copy-done.1
  3.0 0.0 copy-start.2
  3.0 1.0 copy-done.2
  4.1 79.3 %gather.1 = (bf16[8192,512]{1,0:T(8,128)(2,1)}, bf16[1024,1792]{1,0:T(8,128)(2,1)S(1)}, bf16[1024,512]{1,0:T(8,128)(2,1)S(1)}) custom-call(bf16[32,8192]{1,0:T(8,128)(2,1)S(1)} %copy-done.2, bf16[256,1792]{1,0:T(8,128)(2,1)S(1)} %copy-done.1, bf16[1024,512]{1,0:T(8,128)(2,1)S(1)} %copy-done), custom_call_target="tpu_custom_call" | custom-call | tf_op jit(solution)/shard_map/gather/pallas_call | solution.py:192
  83.4 36.6 %step.1 = (bf16[8192,1792]{1,0:T(8,128)(2,1)}, f32[512,1792]{1,0:T(8,128)}, f32[512,1792]{1,0:T(8,128)}) custom-call(bf16[8192,512]{1,0:T(8,128)(2,1)} %get-tuple-element.6.basis_ref, bf16[1024,512]{1,0:T(8,128)(2,1)S(1)} %get-tuple-element.7.red_ref, bf16[1024,1792]{1,0:T(8,128)(2,1)S(1)} %get-tuple-element.8.og_ref, f32[512,1792]{1,0:T(8,128)} %first_ref.1, ...), custom_call_target="tpu_custom_call" | custom-call | tf_op jit(solution)/shard_map/step/pallas_call | solution.py:246
Async XLA Ops:
  0.6 1.2 %copy-start = (bf16[1024,512]{1,0:T(8,128)(2,1)S(1)}, bf16[1024,512]{1,0:T(8,128)(2,1)}, u32[]{:S(2)}) copy-start(bf16[1024,512]{1,0:T(8,128)(2,1)} %basis_ref.1) | copy-start | bytes 3145732
  1.9 1.2 copy-start.1
  3.0 1.0 copy-start.2

commit v2 on v1

v2 whole, which is shorter than its diff:
```python
import functools
import itertools

import jax
import jax.numpy as jnp
from jax import lax
from jax.experimental import pallas as pl
from jax.experimental.pallas import tpu as pltpu
from jax.sharding import PartitionSpec as P

STEP = 10
MESH = pl.DeviceIdType.MESH


def flip(index, stride):
    return index + stride - 2 * stride * lax.rem(lax.div(index, stride), 2)


def counts_of(n_dp, n_mp):
    hops = 4 * (n_mp // 2 - 1)
    both = 2 * (n_dp - 1)
    return hops, 1 + both + (n_mp - 1) + both + (n_dp - 1)


def gather_kernel(
    n_dp, n_mp, act_ref, og_ref, basis_ref, basis_out, og_out, red_out,
    act, bas, og, red, acc, send, recv, hop_send, hop_recv, local,
):
    q, m = lax.axis_index("dp"), lax.axis_index("mp")
    chips = n_mp // 2
    z, c = lax.div(m, 2), lax.rem(m, 2)
    twin = (q, 2 * z + 1 - c)
    strides = [1 << s for s in range(n_dp.bit_length() - 1)]
    orders = [strides, strides[::-1]]
    rows = basis_ref.shape[0]
    piece = rows // 4
    tokens = og_ref.shape[0]
    mine = act_ref.shape[0]

    load_act = pltpu.make_async_copy(act_ref, act, local.at[5])
    load_act.start()
    own_basis = pltpu.make_async_copy(basis_ref, bas.at[pl.ds(pl.multiple_of(m * rows, 128), rows), :], local.at[0])
    own_basis.start()
    own_og = pltpu.make_async_copy(og_ref, og.at[pl.ds(pl.multiple_of(q * tokens, 128), tokens), :], local.at[1])
    own_og.start()

    barrier = pltpu.get_barrier_semaphore()
    for k in range(1, n_mp):
        pl.semaphore_signal(barrier, inc=1, device_id=(q, lax.rem(m + k, n_mp)), device_id_type=MESH)
    for stride in strides:
        pl.semaphore_signal(barrier, inc=1, device_id=(flip(q, stride), m), device_id_type=MESH)
    pl.semaphore_wait(barrier, n_mp - 1 + len(strides))

    numbers = itertools.count()
    sent = []

    def push(src, dst, device):
        i = next(numbers)
        copy = pltpu.make_async_remote_copy(
            src_ref=src, dst_ref=dst, send_sem=send.at[i], recv_sem=recv.at[i],
            device_id=device, device_id_type=MESH,
        )
        copy.start()
        sent.append(copy)
        return copy

    def part(ref, start, size):
        return ref.at[pl.ds(pl.multiple_of(start, 16), size), :]

    def stage(ref, base, step, size, half, held, s):
        stride = orders[half][s]
        partner = (flip(q, stride), m)
        copies = []
        for b in held:
            where = part(ref, base + b * step + half * size, size)
            copies.append(push(where, where, partner))
        return copies, held + [flip(b, stride) for b in held]

    parity = lax.rem(lax.rem(q, 2) + lax.rem(lax.div(q, 2), 2), 2)
    neighbours = [(flip(q, 1), m), (flip(q, 2), m)]
    ways = [1, -1]

    def hop(kind, way, t, j, shard_z, half_number, device):
        i = (way * (chips - 1) + t) * 2 + j
        where = part(bas, (2 * shard_z + c) * rows + half_number * 2 * piece + j * piece, piece)
        return pltpu.make_async_remote_copy(
            src_ref=where, dst_ref=where, send_sem=hop_send.at[kind, i],
            recv_sem=hop_recv.at[kind, i], device_id=device, device_id_type=MESH,
        )

    def gives(way, t):
        if way == 0:
            return jnp.logical_and(z < chips - 1, z - t >= 0), z - t
        return jnp.logical_and(z > 0, z + t <= chips - 1), z + t

    def gets(way, t):
        if way == 0:
            return z - 1 - t >= 0, z - 1 - t
        return z + 1 + t <= chips - 1, z + 1 + t

    def along(way, t, j):
        return hop(0, way, t, j, gives(way, t)[1], parity, (q, m + 2 * ways[way]))

    def along_in(way, t, j):
        return hop(0, way, t, j, gets(way, t)[1], parity, (q, m - 2 * ways[way]))

    def across(way, t, j):
        return hop(1, way, t, j, gets(way, t)[1], parity, neighbours[j])

    def across_in(way, t, j):
        return hop(1, way, t, j, gets(way, t)[1], 1 - parity, neighbours[j])

    def over(kind, way, t, j):
        half_number = parity if kind == 2 else 1 - parity
        return hop(kind, way, t, j, gets(way, t)[1], half_number, twin)

    def over_in(kind, way, t, j):
        half_number = parity if kind == 2 else 1 - parity
        i = (way * (chips - 1) + t) * 2 + j
        start = (2 * gets(way, t)[1] + 1 - c) * rows + half_number * 2 * piece + j * piece
        where = part(bas, start, piece)
        return pltpu.make_async_remote_copy(
            src_ref=where, dst_ref=where, send_sem=hop_send.at[kind, i],
            recv_sem=hop_recv.at[kind, i], device_id=twin, device_id_type=MESH,
        )

    own = m * rows
    own_basis.wait()
    for j in range(2):
        for way in range(2):
            @pl.when(gives(way, 0)[0])
            def _(way=way, j=j):
                along(way, 0, j).start()

    og_half = tokens // 2
    og_held, og_copies = [[q], [q]], [[], []]
    own_og.wait()
    for h in range(2):
        og_copies[h], og_held[h] = stage(og, 0, tokens, og_half, h, og_held[h], 0)
    twin_own = push(part(bas, own, rows), part(bas, own, rows), twin)

    def add(start):
        where = pl.multiple_of(start, 128)
        acc[...] += jnp.dot(
            act[:, pl.ds(where, rows)], bas[pl.ds(where, rows), :],
            preferred_element_type=jnp.float32,
        )

    acc[...] = jnp.zeros_like(acc)
    load_act.wait()
    add(own)

    def arrive(t):
        for j in range(2):
            for way in range(2):
                @pl.when(gets(way, t)[0])
                def _(way=way, j=j):
                    along_in(way, t, j).wait_recv()
                if t + 1 < chips - 1:
                    @pl.when(gives(way, t + 1)[0])
                    def _(way=way, j=j):
                        along(way, t + 1, j).start()
                @pl.when(gets(way, t)[0])
                def _(way=way, j=j):
                    across(way, t, j).start()
                    over(2, way, t, j).start()

    def settle(t):
        for way in range(2):
            @pl.when(gets(way, t)[0])
            def _(way=way):
                for j in range(2):
                    across_in(way, t, j).wait_recv()
                    over(3, way, t, j).start()
                add((2 * gets(way, t)[1] + c) * rows)

    arrive(0)
    for s in range(1, len(strides)):
        for h in range(2):
            for copy in og_copies[h]:
                copy.wait_recv()
            og_copies[h], og_held[h] = stage(og, 0, tokens, og_half, h, og_held[h], s)
    twin_own.wait_recv()
    add((2 * z + 1 - c) * rows)
    for t in range(1, chips - 1):
        arrive(t)
        settle(t - 1)
    settle(chips - 2)
    for t in range(chips - 1):
        for way in range(2):
            @pl.when(gets(way, t)[0])
            def _(way=way, t=t):
                for kind in (2, 3):
                    for j in range(2):
                        over_in(kind, way, t, j).wait_recv()
                add((2 * gets(way, t)[1] + 1 - c) * rows)

    place = q * tokens + m * mine
    red[pl.ds(pl.multiple_of(place, 16), mine), :] = acc[...].astype(red.dtype)
    group_copies = []
    for k in range(1, n_mp):
        where = part(red, place, mine)
        group_copies.append(push(where, where, (q, lax.rem(m + k, n_mp))))
    out_basis = pltpu.make_async_copy(bas, basis_out, local.at[2])
    out_basis.start()
    for copy in group_copies:
        copy.wait_recv()
    quarter = tokens // 4
    side = c * (tokens // 2)
    red_held, red_copies = [[q], [q]], [[], []]
    for s in range(len(strides)):
        for h in range(2):
            for copy in red_copies[h]:
                copy.wait_recv()
            red_copies[h], red_held[h] = stage(red, side, tokens, quarter, h, red_held[h], s)
    for h in range(2):
        for copy in red_copies[h]:
            copy.wait_recv()
    last = []
    for k in range(1, n_dp):
        where = part(red, lax.rem(q + k, n_dp) * tokens + side, tokens // 2)
        last.append(push(where, where, twin))
    for h in range(2):
        for copy in og_copies[h]:
            copy.wait_recv()
    out_og = pltpu.make_async_copy(og, og_out, local.at[3])
    out_og.start()
    for copy in last:
        copy.wait_recv()
    out_red = pltpu.make_async_copy(red, red_out, local.at[4])
    out_red.start()
    for copy in sent:
        copy.wait_send()
    for t in range(chips - 1):
        for way in range(2):
            @pl.when(gives(way, t)[0])
            def _(way=way, t=t):
                for j in range(2):
                    along(way, t, j).wait_send()
            @pl.when(gets(way, t)[0])
            def _(way=way, t=t):
                for j in range(2):
                    across(way, t, j).wait_send()
                    over(2, way, t, j).wait_send()
                    over(3, way, t, j).wait_send()
    out_basis.wait()
    out_og.wait()
    out_red.wait()


def gather(activations, out_grads, basis):
    n_dp, n_mp = lax.axis_size("dp"), lax.axis_size("mp")
    mine, width = activations.shape
    tokens, columns = out_grads.shape
    rank = basis.shape[1]
    hops, count = counts_of(n_dp, n_mp)
    anywhere = pl.BlockSpec(memory_space=pl.ANY)
    shapes = [(width, rank), (n_dp * tokens, columns), (n_dp * tokens, rank)]
    return pl.pallas_call(
        functools.partial(gather_kernel, n_dp, n_mp),
        out_shape=[jax.ShapeDtypeStruct(shape, jnp.bfloat16) for shape in shapes],
        in_specs=[anywhere] * 3,
        out_specs=[anywhere] * 3,
        scratch_shapes=[pltpu.VMEM(shape, jnp.bfloat16) for shape in [(mine, width)] + shapes]
        + [
            pltpu.VMEM((mine, rank), jnp.float32),
            pltpu.SemaphoreType.DMA((count,)),
            pltpu.SemaphoreType.DMA((count,)),
            pltpu.SemaphoreType.DMA((4, hops)),
            pltpu.SemaphoreType.DMA((4, hops)),
            pltpu.SemaphoreType.DMA((6,)),
        ],
        compiler_params=pltpu.CompilerParams(
            collective_id=0, has_side_effects=True, vmem_limit_bytes=58 * 2**20
        ),
        name="gather",
    )(activations, out_grads, basis)


def step_kernel(
    groups, blocks, basis_ref, red_ref, og_ref, first_ref, second_ref, update_ref, new_first_ref,
    new_second_ref, turned, normalized,
):
    i = pl.program_id(0)
    block = og_ref.shape[1]

    @pl.when(i == 0)
    def _():
        turned[...] = red_ref[...].T

    @pl.when(i < blocks)
    def _():
        projected = jnp.dot(turned[...], og_ref[...], preferred_element_type=jnp.float32) / groups
        new_first = 0.9 * first_ref[...] + 0.1 * projected
        new_second = 0.999 * second_ref[...] + 0.001 * projected * projected
        new_first_ref[...] = new_first
        new_second_ref[...] = new_second
        first_hat = new_first / (1.0 - 0.9**STEP)
        second_hat = new_second / (1.0 - 0.999**STEP)
        normalized[:, pl.ds(pl.multiple_of(i * block, block), block)] = (
            first_hat / (jnp.sqrt(second_hat) + 1e-08)
        ).astype(jnp.bfloat16)

    @pl.when(i >= blocks)
    def _():
        update_ref[...] = jnp.dot(
            basis_ref[...], normalized[...], preferred_element_type=jnp.float32
        ).astype(update_ref.dtype)


def step(basis, red, og, first, second, groups):
    rank, columns = first.shape
    width, tokens = basis.shape[0], og.shape[0]
    block = next(b for b in (columns // 2, 256, 128) if b % 128 == 0 and columns % b == 0)
    blocks = columns // block
    high = min(width, 1024)
    row = lambda n: pl.BlockSpec((high, n), lambda i: (jnp.maximum(i - blocks, 0), 0))
    column = lambda n: pl.BlockSpec((n, block), lambda i: (0, jnp.minimum(i, blocks - 1)))
    return pl.pallas_call(
        functools.partial(step_kernel, groups, blocks),
        grid=(blocks + width // high,),
        out_shape=[
            jax.ShapeDtypeStruct((width, columns), jnp.bfloat16),
            jax.ShapeDtypeStruct(first.shape, jnp.float32),
            jax.ShapeDtypeStruct(second.shape, jnp.float32),
        ],
        in_specs=[
            row(rank),
            pl.BlockSpec((tokens, rank), lambda i: (0, 0), pipeline_mode=pl.Buffered(1)),
            column(tokens), column(rank), column(rank),
        ],
        out_specs=[row(columns), column(rank), column(rank)],
        scratch_shapes=[
            pltpu.VMEM((rank, tokens), jnp.bfloat16), pltpu.VMEM((rank, columns), jnp.bfloat16)
        ],
        compiler_params=pltpu.CompilerParams(vmem_limit_bytes=48 * 2**20),
        name="step",
    )(basis, red, og, first, second)


def body(activations, out_grads, basis, first_moment, second_moment):
    whole_basis, whole_grads, reduced = gather(activations, out_grads, basis)
    return tuple(step(
        whole_basis, reduced, whole_grads, first_moment, second_moment, lax.axis_size("dp")
    ))


def solution(mesh):
    return jax.shard_map(
        body,
        mesh=mesh,
        in_specs=(
            P(("dp", "mp"), None),
            P("dp", "mp"),
            P("mp", None),
            P(None, "mp"),
            P(None, "mp"),
        ),
        out_specs=(P(None, "mp"), P(None, "mp"), P(None, "mp")),
        check_vma=False,
    )
```

time: 120 us -> 108 us (0.900)
  the two profiles are of different devices: /device:TPU:25 before, /device:TPU:1 now
where the time goes in v2:
time: 108 us
  Pallas kernels  104 us (96%)
  local copies, waits for them, and re-layouts  3.26 us (3%)
    pallas_call x1, Pallas kernels, gather(): pl.pallas_call(functools.partial(gather_kernel, n_dp, n_mp), out_shape=[j...  76.2 us
    pallas_call x1, Pallas kernels, step(): pl.pallas_call(functools.partial(step_kernel, groups, blocks), grid=(bloc...  27.5 us
    unnamed x4, local copies, waits for them, and re-layouts  3.26 us

profile of v2, /device:TPU:1, one launch (start us, length us, event | category | flops | bytes accessed | tf_op | source)
XLA Modules:
  0.0 107.6 jit_solution(4812301583671540946)
XLA Ops:
  0.6 76.2 %gather.1 = (bf16[8192,512]{1,0:T(8,128)(2,1)}, bf16[1024,1792]{1,0:T(8,128)(2,1)}, bf16[1024,512]{1,0:T(8,128)(2,1)}) custom-call(bf16[32,8192]{1,0:T(8,128)(2,1)} %act_ref.1, bf16[256,1792]{1,0:T(8,128)(2,1)} %og_ref.1, bf16[1024,512]{1,0:T(8,128)(2,1)} %basis_ref.1), custom_call_target="tpu_custom_call" | custom-call | tf_op jit(solution)/shard_map/gather/pallas_call | solution.py:259
  76.8 0.0 copy-start
  76.8 2.0 %copy-done = bf16[1024,1792]{1,0:T(8,128)(2,1)S(1)} copy-done((bf16[1024,1792]{1,0:T(8,128)(2,1)S(1)}, bf16[1024,1792]{1,0:T(8,128)(2,1)}, u32[]{:S(2)}) %copy-start) | copy-done | bytes 3670040
  78.9 0.0 copy-start.1
  78.9 1.2 %copy-done.1 = bf16[1024,512]{1,0:T(8,128)(2,1)S(1)} copy-done((bf16[1024,512]{1,0:T(8,128)(2,1)S(1)}, bf16[1024,512]{1,0:T(8,128)(2,1)}, u32[]{:S(2)}) %copy-start.1) | copy-done | bytes 1048600
  80.1 27.5 %step.1 = (bf16[8192,1792]{1,0:T(8,128)(2,1)}, f32[512,1792]{1,0:T(8,128)}, f32[512,1792]{1,0:T(8,128)}) custom-call(bf16[8192,512]{1,0:T(8,128)(2,1)} %get-tuple-element.6.basis_ref, bf16[1024,512]{1,0:T(8,128)(2,1)S(1)} %copy-done.1, bf16[1024,1792]{1,0:T(8,128)(2,1)S(1)} %copy-done, f32[512,1792]{1,0:T(8,128)} %first_ref.1, f32[512,1792]{1,0:T(8,128)} %second_ref.1), custom_call_target="tpu_custom_call" | custom-call | tf_op jit(solution)/shard_map/step/pallas_call | solution.py:319
Async XLA Ops:
  76.8 2.0 %copy-start = (bf16[1024,1792]{1,0:T(8,128)(2,1)S(1)}, bf16[1024,1792]{1,0:T(8,128)(2,1)}, u32[]{:S(2)}) copy-start(bf16[1024,1792]{1,0:T(8,128)(2,1)} %get-tuple-element.8.og_ref) | copy-start | bytes 11010052
  78.9 1.2 %copy-start.1 = (bf16[1024,512]{1,0:T(8,128)(2,1)S(1)}, bf16[1024,512]{1,0:T(8,128)(2,1)}, u32[]{:S(2)}) copy-start(bf16[1024,512]{1,0:T(8,128)(2,1)} %get-tuple-element.7.red_ref) | copy-start | bytes 3145732

commit v3 on v2

--- a/solution.py
+++ b/solution.py
@@ -176,7 +176,7 @@
 
     arrive(0)
     for s in range(1, len(strides)):
-        for h in range(2):
+        for h in (0,):
             for copy in og_copies[h]:
                 copy.wait_recv()
             og_copies[h], og_held[h] = stage(og, 0, tokens, og_half, h, og_held[h], s)
@@ -186,6 +186,11 @@
         arrive(t)
         settle(t - 1)
     settle(chips - 2)
+    for s in range(1, len(strides)):
+        for h in (1,):
+            for copy in og_copies[h]:
+                copy.wait_recv()
+            og_copies[h], og_held[h] = stage(og, 0, tokens, og_half, h, og_held[h], s)
     for t in range(chips - 1):
         for way in range(2):
             @pl.when(gets(way, t)[0])
@@ -333,7 +338,7 @@
         scratch_shapes=[
             pltpu.VMEM((rank, tokens), jnp.bfloat16), pltpu.VMEM((rank, columns), jnp.bfloat16)
         ],
-        compiler_params=pltpu.CompilerParams(vmem_limit_bytes=48 * 2**20),
+        compiler_params=pltpu.CompilerParams(vmem_limit_bytes=60 * 2**20),
         name="step",
     )(basis, red, og, first, second)
 

time: 108 us -> 116 us (1.074)
  Pallas kernels: 104 us -> 115 us
  local copies, waits for them, and re-layouts: 3.26 us -> 0 us
    pallas_call x1, Pallas kernels: 76.2 us -> 86.4 us  [gather(): pl.pallas_call(functools.partial(gather_kernel, n_dp, n_mp), out_shape=[j...]
    unnamed x4 -> x0, local copies, waits for them, and re-layouts: 3.26 us -> none
    pallas_call x1, Pallas kernels: 27.5 us -> 28.8 us  [step(): pl.pallas_call(functools.partial(step_kernel, groups, blocks), grid=(bloc...]
where the time goes in v3:
time: 116 us
  Pallas kernels  115 us (99%)
    pallas_call x1, Pallas kernels, gather(): pl.pallas_call(functools.partial(gather_kernel, n_dp, n_mp), out_shape=[j...  86.4 us
    pallas_call x1, Pallas kernels, step(): pl.pallas_call(functools.partial(step_kernel, groups, blocks), grid=(bloc...  28.8 us

profile of v3, /device:TPU:1, one launch (start us, length us, event | category | flops | bytes accessed | tf_op | source)
XLA Modules:
  0.0 115.9 jit_solution(576938450097873271)
XLA Ops:
  0.6 86.4 %gather.1 = (bf16[8192,512]{1,0:T(8,128)(2,1)}, bf16[1024,1792]{1,0:T(8,128)(2,1)}, bf16[1024,512]{1,0:T(8,128)(2,1)}) custom-call(bf16[32,8192]{1,0:T(8,128)(2,1)} %act_ref.1, bf16[256,1792]{1,0:T(8,128)(2,1)} %og_ref.1, bf16[1024,512]{1,0:T(8,128)(2,1)} %basis_ref.1), custom_call_target="tpu_custom_call" | custom-call | tf_op jit(solution)/shard_map/gather/pallas_call | solution.py:264
  87.0 28.8 %step.1 = (bf16[8192,1792]{1,0:T(8,128)(2,1)}, f32[512,1792]{1,0:T(8,128)}, f32[512,1792]{1,0:T(8,128)}) custom-call(bf16[8192,512]{1,0:T(8,128)(2,1)} %get-tuple-element.6.basis_ref, bf16[1024,512]{1,0:T(8,128)(2,1)} %get-tuple-element.7.red_ref, bf16[1024,1792]{1,0:T(8,128)(2,1)} %get-tuple-element.8.og_ref, f32[512,1792]{1,0:T(8,128)} %first_ref.1, ...), custom_call_target="tpu_custom_call" | custom-call | tf_op jit(solution)/shard_map/step/pallas_call | solution.py:324
